TPU v7x, 32 devices: a whole 2x2x4 slice. The times are simulated.
32 devices in a mesh: grp: 2 (over x), azi: 4 (over y, core), pln: 4 (over z).
Axes of the slice: x: 2, y: 2, z: 4, core: 2. Of those that a mesh axis runs over, the one named last changes fastest.
Arguments:
- fields: float32 [5, 16, 128, 1024], P(None, 'grp', 'pln', 'azi'), parts along dimension 1, may hold values from -8 to 8
- swirl_cfl: float32 [16, 128, 1024], P('grp', 'pln', 'azi'), parts along dimension 0, may hold values from 1 to 32768
Outputs:
- advanced: float32 [5, 16, 128, 1024], P(None, 'grp', 'pln', 'azi'), parts along dimension 1
There are 2 independent parts, one for each index of `grp`. A program takes and returns all parts, laid end to end along the dimension named above; each array names one. Nothing has to cross between parts.
All inputs are finite; a program needn't handle non-finite values.
Results may differ from a plain program's by a relative error of at most 0.000082.
Values sent between devices are 32-bit elements; how exact they have to be, the bound alone decides.
A program may use at most 64 MiB of HBM per device.

v0:
```python
import jax
import jax.numpy as jnp
from jax import lax
from jax.sharding import PartitionSpec as P

INNER_A = 7.0 / 9.0
INNER_B = 1.0 / 36.0
MEAN_MACH = 0.4
SECTION_STEP = 0.25
HIGHEST = lax.Precision.HIGHEST
margin_cells = 20


def padded(array, sides, width):
    for axis, dim in sides:
        size, length = (lax.axis_size(axis), array.shape[dim])
        up = [(i, (i + 1) % size) for i in range(size)]
        down = [(j, i) for i, j in up]
        last = lax.slice_in_dim(array, length - width, length, axis=dim)
        first = lax.slice_in_dim(array, 0, width, axis=dim)
        before = lax.ppermute(last, axis, up)
        after = lax.ppermute(first, axis, down)
        array = jnp.concatenate([before, array, after], axis=dim)
    return array


def from_behind(block, axis, distance):
    devices = range(lax.axis_size(axis))
    route = [((i - distance) % len(devices), i) for i in devices]
    return lax.ppermute(block, axis, route)


def compact_rows(global_idx, row_count, periodic):
    filler = jnp.zeros(global_idx.shape, jnp.float32)
    lower_diag = filler + 1.0 / 3.0
    upper_diag = filler + 1.0 / 3.0
    stencil = [filler - INNER_B, filler - INNER_A, filler, filler + INNER_A, filler + INNER_B]
    if not periodic:
        near_edge = (global_idx == 1) | (global_idx == row_count - 2)
        first_row = global_idx == 0
        final_row = global_idx == row_count - 1
        outside = (global_idx < 0) | (global_idx >= row_count)
        near_taps = (0.0, -0.75, 0.0, 0.75, 0.0)
        first_taps = (0.0, 0.0, -2.5, 2.0, 0.5)
        final_taps = (-0.5, -2.0, 2.5, 0.0, 0.0)
        lower_diag = jnp.where(
            near_edge,
            0.25,
            jnp.where(first_row | outside, 0.0, jnp.where(final_row, 2.0, lower_diag)),
        )
        upper_diag = jnp.where(
            near_edge,
            0.25,
            jnp.where(final_row | outside, 0.0, jnp.where(first_row, 2.0, upper_diag)),
        )
        stencil = [
            jnp.where(
                outside,
                0.0,
                jnp.where(
                    near_edge,
                    near_taps[tap_index],
                    jnp.where(
                        first_row,
                        first_taps[tap_index],
                        jnp.where(final_row, final_taps[tap_index], stencil[tap_index]),
                    ),
                ),
            )
            for tap_index in range(5)
        ]
    return (lower_diag, upper_diag, stencil)


def compact_matrix(global_idx, row_count, periodic):
    lower_diag, upper_diag, stencil = compact_rows(global_idx, row_count, periodic)
    length = global_idx.shape[0]
    lower_diag = lower_diag.at[0].set(0.0)
    upper_diag = upper_diag.at[length - 1].set(0.0)
    row_ids = lax.broadcasted_iota(jnp.int32, (length, length), 0)
    col_ids = lax.broadcasted_iota(jnp.int32, (length, length), 1)
    explicit = jnp.zeros((length, length), jnp.float32)
    for offset in range(-2, 3):
        explicit = explicit + jnp.where(
            col_ids == row_ids + offset, stencil[offset + 2][:, None], 0.0
        )
    diagonal = jnp.ones((length,), jnp.float32)
    return lax.linalg.tridiagonal_solve(lower_diag, diagonal, upper_diag, explicit)


def compose(earlier_map, later_map):
    return (later_map[0] * earlier_map[0], later_map[0] * earlier_map[1] + later_map[1])


def block_recurrence(swirl_cfl, source):
    azim_dev = swirl_cfl.shape[-1]
    span = 128
    pieces = azim_dev // span
    row_ids = lax.broadcasted_iota(jnp.int32, (span, span), 0)
    col_ids = lax.broadcasted_iota(jnp.int32, (span, span), 1)
    running = jnp.where(row_ids <= col_ids, 1.0, 0.0).astype(jnp.float32)
    log_rate = -jnp.log1p(1.0 / swirl_cfl)
    lead_shape = log_rate.shape[:-1]
    log_rate = log_rate.reshape(lead_shape + (pieces, span))
    cumulative = jnp.einsum("rxks,st->rxkt", log_rate, running, precision=HIGHEST)
    rate_local = jnp.exp(cumulative)
    shaped = source.reshape(source.shape[:-1] + (pieces, span))
    scaled = shaped * jnp.exp(-cumulative)[None]
    summed = jnp.einsum("frxks,st->frxkt", scaled, running, precision=HIGHEST)
    source_local = rate_local[None] * summed
    rate_parts = [rate_local[..., 0, :]]
    source_parts = [source_local[..., 0, :]]
    rate_here = rate_local[..., 1, :]
    rate_end = rate_parts[-1][..., -1:]
    source_end = source_parts[-1][..., -1:]
    rate_parts.append(rate_here * rate_end)
    source_parts.append(rate_here[None] * source_end + source_local[..., 1, :])
    rate_cum = jnp.concatenate(rate_parts, axis=-1)[None]
    source_cum = jnp.concatenate(source_parts, axis=-1)
    return (rate_cum, source_cum)


def local(fields, swirl_cfl):
    plane_count = fields.shape[1]
    axial_dev = fields.shape[2]
    azim_dev = fields.shape[3]
    radial_matrix = compact_matrix(jnp.arange(plane_count, dtype=jnp.int32), plane_count, False)
    d_radial = jnp.einsum(
        "rs,fsxt->frxt", radial_matrix, jnp.stack([fields[2], fields[4]]), precision=HIGHEST
    )
    azim_pair = padded(fields[3:5], (("azi", 3),), margin_cells)
    azim_span = azim_dev + 2 * margin_cells
    azim_matrix = compact_matrix(jnp.arange(azim_span, dtype=jnp.int32), azim_span, True)[
        margin_cells : margin_cells + azim_dev
    ]
    d_azim = jnp.einsum("frxe,te->frxt", azim_pair, azim_matrix, precision=HIGHEST)
    axial_total = axial_dev * lax.axis_size("pln")
    axial_matrix = compact_matrix(jnp.arange(axial_total, dtype=jnp.int32), axial_total, False)
    pencils_dx = jnp.einsum(
        "frxt,yx->fryt",
        lax.all_to_all(fields, "pln", split_axis=1, concat_axis=2, tiled=True),
        axial_matrix,
        precision=HIGHEST,
    )
    d_axial = lax.all_to_all(pencils_dx, "pln", split_axis=2, concat_axis=1, tiled=True)
    drift_terms = MEAN_MACH * d_axial
    divergence = d_axial[1] + d_radial[0] + d_azim[0]
    tendency = jnp.stack(
        [
            -drift_terms[0] - divergence,
            -drift_terms[1] - d_axial[4],
            -drift_terms[2] - d_radial[1],
            -drift_terms[3] - d_azim[1],
            -drift_terms[4] - divergence,
        ]
    )
    sectioned = fields + SECTION_STEP * tendency
    weight = 1.0 / (1.0 + swirl_cfl)
    source = sectioned * weight[None]
    rate_cum, source_cum = block_recurrence(swirl_cfl, source)
    block_maps = jnp.concatenate([rate_cum[..., -1], source_cum[..., -1]], axis=0)

    def relay(turn_index, relay_state):
        message, combined = relay_state
        message = from_behind(message, "azi", -1)
        joined = compose((combined[:1], combined[1:]), (message[:1], message[1:]))
        return (message, jnp.concatenate(joined, axis=0))

    unused, combined = lax.fori_loop(0, lax.axis_size("azi") - 1, relay, (block_maps, block_maps))
    incoming = combined[1:] / (1.0 - combined[:1])
    return rate_cum * incoming[..., None] + source_cum


def solution(mesh):
    placed = (P(None, "grp", "pln", "azi"), P("grp", "pln", "azi"))
    return jax.shard_map(
        local, mesh=mesh, in_specs=placed, out_specs=P(None, "grp", "pln", "azi"), check_vma=False
    )
```

profile of v0, /device:TPU:0, one launch (start us, length us, event | category | flops | bytes accessed | tf_op | source)
XLA Modules:
  0.0 730.2 jit_solution(8496393668793324750)
XLA Ops:
  0.0 2.5 copy.41
  2.5 6.4 all-to-all-start
  11.9 195.6 %while.84 = (s32[]{:T(128)}, f32[]{:T(128)}, f32[128]{0:T(128)S(1)}, f32[3,32]{1,0:T(4,128)S(1)}, f32[3,32,128]{2,1,0:T(8,128)S(1)}, /*index=5*/f32[3,32]{1,0:T(...) while((s32[]{:T(128)}, f32[]{:T(128)}, ...), condition=%wide.region_1.2_spmd, body=%wide.region_0.1_spmd.sunk | while | flops 12417 | bytes 103669 | solution.py:88
  55.9 20.4 %fusion.550 = (f32[128]{0:T(128)S(1)}, f32[128]{0:T(128)S(1)}, f32[128]{0:T(128)S(1)}, f32[128]{0:T(128)S(1)}, f32[128]{0:T(128)S(1)}, /*index=5*/f32[128]{0:T(1...) fusion(f32[3,32,128]{2,1,0:T(8,128)S(1)} %get-tuple-element.195, ...), kind=kLoop, calls=%fused_computation.40.clone.1 | loop fusion | flops 12288 | bytes 33664 | tf_op jit(solution)/shard_map/while/body/eval_jaxpr/div | solution.py:88
  121.1 20.4 %fusion.550 = (f32[128]{0:T(128)S(1)}, f32[128]{0:T(128)S(1)}, f32[128]{0:T(128)S(1)}, f32[128]{0:T(128)S(1)}, f32[128]{0:T(128)S(1)}, /*index=5*/f32[128]{0:T(1...) fusion(f32[3,32,128]{2,1,0:T(8,128)S(1)} %get-tuple-element.195, ...), kind=kLoop, calls=%fused_computation.40.clone.1 | loop fusion | flops 12288 | bytes 33664 | tf_op jit(solution)/shard_map/while/body/eval_jaxpr/div | solution.py:88
  186.3 20.4 %fusion.550 = (f32[128]{0:T(128)S(1)}, f32[128]{0:T(128)S(1)}, f32[128]{0:T(128)S(1)}, f32[128]{0:T(128)S(1)}, f32[128]{0:T(128)S(1)}, /*index=5*/f32[128]{0:T(1...) fusion(f32[3,32,128]{2,1,0:T(8,128)S(1)} %get-tuple-element.195, ...), kind=kLoop, calls=%fused_computation.40.clone.1 | loop fusion | flops 12288 | bytes 33664 | tf_op jit(solution)/shard_map/while/body/eval_jaxpr/div | solution.py:88
  251.0 19.5 %fusion.351 = (f32[128]{0:T(128)S(1)}, f32[128]{0:T(128)S(1)}, f32[128]{0:T(128)S(1)}, f32[128]{0:T(128)S(1)}, f32[128]{0:T(128)S(1)}, /*index=5*/f32[128]{0:T(1...) fusion(f32[128,128]{1,0:T(8,128)S(1)} %select_add_fusion.1, ...), kind=kLoop, calls=%fused_computation.684 | loop fusion | flops 11904 | bytes 32504 | tf_op jit(solution)/shard_map/eval_jaxpr/div | solution.py:88
  271.5 65.1 %while.85 = (s32[]{:T(128)}, f32[128]{0:T(128)S(1)}, f32[3,32,128]{2,1,0:T(8,128)S(1)}, f32[3,32,128]{2,1,0:T(8,128)S(1)}, f32[3,32]{1,0:T(4,128)S(1)}, /*index=...) while((s32[]{:T(128)}, f32[128]{0:T(128)S(1)}, ...), condition=%wide.region_3.4_spmd, body=%wide.region_2.3_spmd.sunk | while | flops 8226 | bytes 101341 | solution.py:88
  272.9 20.1 %fusion.553 = (f32[128]{0:T(128)S(1)}, f32[128]{0:T(128)S(1)}, f32[128]{0:T(128)S(1)}, f32[128]{0:T(128)S(1)}, f32[128]{0:T(128)S(1)}, /*index=5*/f32[128]{0:T(1...) fusion(f32[3,32,128]{2,1,0:T(8,128)S(1)} %get-tuple-element.207, ...), kind=kLoop, calls=%fused_computation.168.clone.1 | loop fusion | flops 8192 | bytes 33536 | tf_op jit(solution)/shard_map/while/body/eval_jaxpr/sub | solution.py:88
  294.6 20.1 %fusion.553 = (f32[128]{0:T(128)S(1)}, f32[128]{0:T(128)S(1)}, f32[128]{0:T(128)S(1)}, f32[128]{0:T(128)S(1)}, f32[128]{0:T(128)S(1)}, /*index=5*/f32[128]{0:T(1...) fusion(f32[3,32,128]{2,1,0:T(8,128)S(1)} %get-tuple-element.207, ...), kind=kLoop, calls=%fused_computation.168.clone.1 | loop fusion | flops 8192 | bytes 33536 | tf_op jit(solution)/shard_map/while/body/eval_jaxpr/sub | solution.py:88
  316.3 20.1 %fusion.553 = (f32[128]{0:T(128)S(1)}, f32[128]{0:T(128)S(1)}, f32[128]{0:T(128)S(1)}, f32[128]{0:T(128)S(1)}, f32[128]{0:T(128)S(1)}, /*index=5*/f32[128]{0:T(1...) fusion(f32[3,32,128]{2,1,0:T(8,128)S(1)} %get-tuple-element.207, ...), kind=kLoop, calls=%fused_computation.168.clone.1 | loop fusion | flops 8192 | bytes 33536 | tf_op jit(solution)/shard_map/while/body/eval_jaxpr/sub | solution.py:88
  337.2 43.5 %while.86 = (s32[]{:T(128)}, f32[]{:T(128)}, f32[296]{0:T(512)S(1)}, f32[9,32]{1,0:T(8,128)S(1)}, f32[9,32,296]{2,1,0:T(8,128)S(1)}, /*index=5*/f32[9,32,296]{2,...) while((s32[]{:T(128)}, f32[]{:T(128)}, ...), condition=%wide.region_5.6_spmd, body=%wide.region_4.5_spmd.sunk | while | flops 28545 | bytes 405261 | solution.py:88
  385.8 222.0 %while.87 = (s32[]{:T(128)}, f32[296]{0:T(512)S(1)}, f32[9,32,296]{2,1,0:T(8,128)S(1)}, f32[9,32,296]{2,1,0:T(8,128)}, f32[9,32]{1,0:T(8,128)S(1)}, /*index=5*/s...) while((s32[]{:T(128)}, f32[296]{0:T(512)S(1)}, ...), condition=%wide.region_7.8_spmd, body=%wide.region_6.7_spmd.sunk | while | flops 18978 | bytes 404097 | solution.py:88
  389.8 20.3 %multiply_subtract_fusion.77 = (f32[296]{0:T(512)S(1)}, f32[296]{0:T(512)S(1)}, f32[296]{0:T(512)S(1)}, f32[296]{0:T(512)S(1)}, f32[296]{0:T(512)S(1)}, /*index=...) fusion(f32[296]{0:T(512)S(1)} %get-tuple-element.1764, ...), kind=kLoop, calls=%fused_computation.364.clone.1 | loop fusion | flops 18944 | bytes 77088 | tf_op jit(solution)/shard_map/while/body/eval_jaxpr/sub | solution.py:88
  414.5 20.3 %multiply_subtract_fusion.77 = (f32[296]{0:T(512)S(1)}, f32[296]{0:T(512)S(1)}, f32[296]{0:T(512)S(1)}, f32[296]{0:T(512)S(1)}, f32[296]{0:T(512)S(1)}, /*index=...) fusion(f32[296]{0:T(512)S(1)} %get-tuple-element.1764, ...), kind=kLoop, calls=%fused_computation.364.clone.1 | loop fusion | flops 18944 | bytes 77088 | tf_op jit(solution)/shard_map/while/body/eval_jaxpr/sub | solution.py:88
  439.2 20.3 %multiply_subtract_fusion.77 = (f32[296]{0:T(512)S(1)}, f32[296]{0:T(512)S(1)}, f32[296]{0:T(512)S(1)}, f32[296]{0:T(512)S(1)}, f32[296]{0:T(512)S(1)}, /*index=...) fusion(f32[296]{0:T(512)S(1)} %get-tuple-element.1764, ...), kind=kLoop, calls=%fused_computation.364.clone.1 | loop fusion | flops 18944 | bytes 77088 | tf_op jit(solution)/shard_map/while/body/eval_jaxpr/sub | solution.py:88
  463.9 20.3 %multiply_subtract_fusion.77 = (f32[296]{0:T(512)S(1)}, f32[296]{0:T(512)S(1)}, f32[296]{0:T(512)S(1)}, f32[296]{0:T(512)S(1)}, f32[296]{0:T(512)S(1)}, /*index=...) fusion(f32[296]{0:T(512)S(1)} %get-tuple-element.1764, ...), kind=kLoop, calls=%fused_computation.364.clone.1 | loop fusion | flops 18944 | bytes 77088 | tf_op jit(solution)/shard_map/while/body/eval_jaxpr/sub | solution.py:88
  488.5 20.3 %multiply_subtract_fusion.77 = (f32[296]{0:T(512)S(1)}, f32[296]{0:T(512)S(1)}, f32[296]{0:T(512)S(1)}, f32[296]{0:T(512)S(1)}, f32[296]{0:T(512)S(1)}, /*index=...) fusion(f32[296]{0:T(512)S(1)} %get-tuple-element.1764, ...), kind=kLoop, calls=%fused_computation.364.clone.1 | loop fusion | flops 18944 | bytes 77088 | tf_op jit(solution)/shard_map/while/body/eval_jaxpr/sub | solution.py:88
  513.0 20.3 %multiply_subtract_fusion.77 = (f32[296]{0:T(512)S(1)}, f32[296]{0:T(512)S(1)}, f32[296]{0:T(512)S(1)}, f32[296]{0:T(512)S(1)}, f32[296]{0:T(512)S(1)}, /*index=...) fusion(f32[296]{0:T(512)S(1)} %get-tuple-element.1764, ...), kind=kLoop, calls=%fused_computation.364.clone.1 | loop fusion | flops 18944 | bytes 77088 | tf_op jit(solution)/shard_map/while/body/eval_jaxpr/sub | solution.py:88
  537.7 20.3 %multiply_subtract_fusion.77 = (f32[296]{0:T(512)S(1)}, f32[296]{0:T(512)S(1)}, f32[296]{0:T(512)S(1)}, f32[296]{0:T(512)S(1)}, f32[296]{0:T(512)S(1)}, /*index=...) fusion(f32[296]{0:T(512)S(1)} %get-tuple-element.1764, ...), kind=kLoop, calls=%fused_computation.364.clone.1 | loop fusion | flops 18944 | bytes 77088 | tf_op jit(solution)/shard_map/while/body/eval_jaxpr/sub | solution.py:88
  562.4 20.3 %multiply_subtract_fusion.77 = (f32[296]{0:T(512)S(1)}, f32[296]{0:T(512)S(1)}, f32[296]{0:T(512)S(1)}, f32[296]{0:T(512)S(1)}, f32[296]{0:T(512)S(1)}, /*index=...) fusion(f32[296]{0:T(512)S(1)} %get-tuple-element.1764, ...), kind=kLoop, calls=%fused_computation.364.clone.1 | loop fusion | flops 18944 | bytes 77088 | tf_op jit(solution)/shard_map/while/body/eval_jaxpr/sub | solution.py:88
  587.1 20.3 %multiply_subtract_fusion.77 = (f32[296]{0:T(512)S(1)}, f32[296]{0:T(512)S(1)}, f32[296]{0:T(512)S(1)}, f32[296]{0:T(512)S(1)}, f32[296]{0:T(512)S(1)}, /*index=...) fusion(f32[296]{0:T(512)S(1)} %get-tuple-element.1764, ...), kind=kLoop, calls=%fused_computation.364.clone.1 | loop fusion | flops 18944 | bytes 77088 | tf_op jit(solution)/shard_map/while/body/eval_jaxpr/sub | solution.py:88
  608.6 2.0 fusion.403
  610.6 2.7 fusion.402
  613.3 2.6 fusion.401
  615.9 2.5 fusion.400
  618.4 2.7 fusion.399
  621.1 2.6 fusion.398
  623.7 2.6 fusion.397
  626.3 2.7 fusion.396
  629.0 2.7 fusion.395
  631.8 2.7 fusion.394
  634.5 2.6 fusion.393
  637.0 2.5 fusion.392
  639.6 2.5 fusion.391
  651.5 2.7 fusion.390
  654.2 2.7 fusion.389
  656.9 2.0 fusion.383
  659.2 3.7 subtract_divide_fusion.40
  665.0 2.1 copy.43
  667.1 5.1 all-to-all-start.1
  681.3 2.2 fusion.224
  683.5 21.3 %all-to-all-done.1 = f32[5,2,128,256]{3,1,0,2:T(2,128)S(1)} async-done(((f32[5,2,128,256]{3,1,0,2:T(2,128)}), f32[5,2,128,256]{3,1,0,2:T(2,128)S(1)}, u32[]{:S(2)}, u32[]{:S(2)}) %all-to-all-start.1) | async-done | bytes 1310752 | tf_op jit(solution)/shard_map/all_to_all | solution.py:145
  709.0 1.8 sub.2047
  710.8 1.8 neg.44
  720.5 8.3 %while.88 = (s32[]{:T(128)}, f32[6,8,32]{2,1,0:T(8,128)S(1)}, f32[6,8,32]{2,1,0:T(8,128)S(1)}, s32[]{:T(128)}) while((s32[]{:T(128)}, f32[6,8,32]{2,1,0:T(8,128)S(1)}, f32[6,8,32]{2,1,0:T(8,128)S(1)}, s32[]{:T(128)}) %tuple.677), condition=%wide.region_9.10_spmd, body=%wide.region_8.9_spmd.sunk | while | flops 4354 | bytes 69725 | solution.py:169
  722.1 1.8 collective-permute-start
  725.5 1.8 collective-permute-start
  (912 shorter events, 123.6 us)
Async XLA Ops:
  2.5 6.5 copy-start
  2.5 661.1 %all-to-all-start = ((f32[5,8,32,256]{3,2,0,1:T(8,128)}), f32[5,8,32,256]{3,2,0,1:T(8,128)S(1)}, u32[]{:S(2)}, u32[]{:S(2)}) async-start(f32[5,8,32,256]{3,2,0,1:T(8,128)} %copy.41), calls=%async_computation | async-start | bytes 2621440 | tf_op jit(solution)/shard_map/all_to_all | solution.py:141
  9.9 670.0 %collective-permute-start.2 = (f32[2,8,32,20]{3,2,1,0:T(8,128)}, f32[2,8,32,20]{3,2,1,0:T(8,128)}, u32[]{:S(2)}, u32[]{:S(2)}) collective-permute-start(f32[2,8,32,20]{3,2,1,0:T(8,128)} %get-tuple-element.914), channel_id=1, source_target_pairs={{4,0},{8,4},{12,8},{0,12},{5,1},{9,5},{13,9},{1,13},{6,2},{10,6},{... | collective-permute-start | bytes 122888 | tf_op jit(solution)/shard_map/ppermute | solution.py:22
  10.5 669.3 %collective-permute-start.1 = (f32[2,8,32,20]{3,2,1,0:T(8,128)}, f32[2,8,32,20]{3,2,1,0:T(8,128)}, u32[]{:S(2)}, u32[]{:S(2)}) collective-permute-start(f32[2,8,32,20]{3,2,1,0:T(8,128)} %get-tuple-element.913), channel_id=1, source_target_pairs={{0,4},{4,8},{8,12},{12,0},{1,5},{5,9},{9,13},{13,1},{2,6},{6,10},{... | collective-permute-start | bytes 122888 | tf_op jit(solution)/shard_map/ppermute | solution.py:21
  207.5 64.0 %copy-start.14 = (f32[3,32,128]{2,1,0:T(8,128)}, f32[3,32,128]{2,1,0:T(8,128)S(1)}, u32[]{:S(2)}) copy-start(f32[3,32,128]{2,1,0:T(8,128)S(1)} %get-tuple-element.425) | copy-start | bytes 147460
  336.6 0.6 copy-start.16
  385.8 273.1 %copy-start.17 = (f32[3,32,128]{2,1,0:T(8,128)S(1)}, f32[3,32,128]{2,1,0:T(8,128)}, u32[]{:S(2)}) copy-start(f32[3,32,128]{2,1,0:T(8,128)} %copy-done.16) | copy-start | bytes 147460
  607.8 55.9 %copy-start.3 = (f32[9,32,296]{2,1,0:T(8,128)}, f32[9,32,296]{2,1,0:T(8,128)S(1)}, u32[]{:S(2)}) copy-start(f32[9,32,296]{2,1,0:T(8,128)S(1)} %get-tuple-element.435) | copy-start | bytes 1022980
  667.1 6.3 copy-start.10
  667.1 8.1 %copy-start.15 = (f32[8,32,256]{2,1,0:T(8,128)S(1)}, f32[8,32,256]{2,1,0:T(8,128)}, u32[]{:S(2)}) copy-start(f32[8,32,256]{2,1,0:T(8,128)} %param.25) | copy-start | bytes 786436
  667.1 37.7 %all-to-all-start.1 = ((f32[5,2,128,256]{3,1,0,2:T(2,128)}), f32[5,2,128,256]{3,1,0,2:T(2,128)S(1)}, u32[]{:S(2)}, u32[]{:S(2)}) async-start(f32[5,2,128,256]{3,1,0,2:T(2,128)} %copy.43), calls=%async_computation.1 | async-start | bytes 2621440 | tf_op jit(solution)/shard_map/all_to_all | solution.py:145
  675.3 2.2 copy-start.11
  675.3 2.2 copy-start.12
  677.5 2.4 slice-start
  679.0 2.3 copy-start.4
  707.7 7.0 copy-start.1
  707.8 7.0 copy-start.2
  714.7 1.0 copy-start.9
  714.7 1.0 copy-start.8
  714.7 1.1 copy-start.7
  715.7 1.0 copy-start.6
  716.7 0.9 copy-start.5
  719.8 9.1 %copy-start.13 = (f32[8,32,256]{2,1,0:T(8,128)S(1)}, f32[8,32,256]{2,1,0:T(8,128)}, u32[]{:S(2)}) copy-start(f32[8,32,256]{2,1,0:T(8,128)} %get-tuple-element.915) | copy-start | bytes 786436
  720.5 1.6 collective-permute-start
  722.1 3.3 collective-permute-start
  725.5 3.3 collective-permute-start
where the time goes:
time: 743 us; the launch traced here: 730 us
  other arithmetic  380 us (51%)
  loops' own time  143 us (19%)
  local copies, waits for them, and re-layouts  110 us (15%)
  between operations  48.2 us (6%)
  waiting for transfers between devices  25.8 us (3%)
  starting transfers between devices  15.8 us (2%)
  matrix products  7.5 us (1%)
    sub x13, other arithmetic, compact_matrix(): lax.linalg.tridiagonal_solve(lower_diag, diagonal, upper_diag, explicit)  244 us
    another operation x4, loops' own time, compact_matrix(): lax.linalg.tridiagonal_solve(lower_diag, diagonal, upper_diag, explicit)  143 us
    div x15, other arithmetic, compact_matrix(): lax.linalg.tridiagonal_solve(lower_diag, diagonal, upper_diag, explicit)  86.8 us
    slice x89, local copies, waits for them, and re-layouts, compact_matrix(): lax.linalg.tridiagonal_solve(lower_diag, diagonal, upper_diag, explicit)  77.1 us
    broadcast_in_dim x18, other arithmetic, compact_matrix(): lax.linalg.tridiagonal_solve(lower_diag, diagonal, upper_diag, explicit)  40.9 us
    all_to_all x1, waiting for transfers between devices, local(): lax.all_to_all(pencils_dx, 'pln', split_axis=2, concat_axis=1, tiled=True)  21.3 us
  transfers between devices with their start and end apart: 7, of which 4 were waited for; matrix products, arithmetic and copies ran while one was open for 65% of the time, Pallas kernels for 0%

commit v1 on v0

v1 whole, which is shorter than its diff:
```python
import functools

import jax
import jax.numpy as jnp
import numpy as np
from jax import lax
from jax.experimental import pallas as pl
from jax.experimental.pallas import tpu as pltpu
from jax.sharding import PartitionSpec as P

INNER_A = 7.0 / 9.0
INNER_B = 1.0 / 36.0
MEAN_MACH = 0.4
SECTION_STEP = 0.25
HIGHEST = lax.Precision.HIGHEST
MESH = pl.DeviceIdType.MESH
F32 = jnp.float32
LANES = 128
CHUNK = 16
SHIFTS = (1, 2, 4, 8, 16, 32, 64)


def line_matrices(n):
    low = np.full(n, 1.0 / 3.0)
    up = np.full(n, 1.0 / 3.0)
    right = np.zeros((n, n))
    for g in range(2, n - 2):
        right[g, g - 2 : g + 3] = (-INNER_B, -INNER_A, 0.0, INNER_A, INNER_B)
    for g in (1, n - 2):
        low[g] = up[g] = 0.25
        right[g, g - 1 : g + 2] = (-0.75, 0.0, 0.75)
    low[0], up[0], low[n - 1], up[n - 1] = 0.0, 2.0, 2.0, 0.0
    right[0, :3] = (-2.5, 2.0, 0.5)
    right[n - 1, n - 3 :] = (-0.5, -2.0, 2.5)
    both = np.concatenate([np.eye(n), right], axis=1)
    pivot = np.ones(n)
    for g in range(1, n):
        factor = low[g] / pivot[g - 1]
        pivot[g] = 1.0 - factor * up[g - 1]
        both[g] -= factor * both[g - 1]
    both[n - 1] /= pivot[n - 1]
    for g in range(n - 2, -1, -1):
        both[g] = (both[g] - up[g] * both[g + 1]) / pivot[g]
    return both[:, :n], both[:, n:]


def axial_constants(planes, cells, count, far):
    n = cells * count
    inverse, matrix = line_matrices(n)
    own = np.zeros((count, planes * cells, planes * cells))
    weights = np.zeros((count, 4 * planes, planes * cells))
    halo = np.zeros((count, planes * cells, (4 + 2 * len(far)) * planes))
    to_right, to_left = {}, {}
    for k in range(count):
        a, b = k * cells, (k + 1) * cells
        if k < count - 1:
            to_right[k] = matrix[b + 1, a:b] / inverse[b + 1, b]
        if k > 0:
            to_left[k] = matrix[a - 2, a:b] / inverse[a - 2, a - 1]
    for k in range(count):
        a, b = k * cells, (k + 1) * cells
        for p in range(planes):
            rows = slice(p * cells, (p + 1) * cells)
            own[k, rows, rows] = matrix[a:b, a:b]
            if k in to_right:
                weights[k, p, rows] = to_right[k]
                weights[k, planes + p, p * cells + cells - 1] = 1.0
            if k in to_left:
                weights[k, 2 * planes + p, rows] = to_left[k]
                weights[k, 3 * planes + p, p * cells] = 1.0
            if k > 0:
                halo[k, rows, p] = inverse[a:b, a]
                halo[k, p * cells, planes + p] = (
                    matrix[a, a - 1] - inverse[a, a] * to_right[k - 1][-1]
                )
            if k < count - 1:
                halo[k, rows, 2 * planes + p] = inverse[a:b, b - 1]
                halo[k, p * cells + cells - 1, 3 * planes + p] = (
                    matrix[b - 1, b] - inverse[b - 1, b - 1] * to_left[k + 1][0]
                )
            for j, d in enumerate(far):
                if k - d >= 0:
                    start = (k - d + 1) * cells
                    halo[k, rows, (4 + j) * planes + p] = inverse[a:b, start]
                if k + d < count:
                    end = (k + d) * cells - 1
                    halo[k, rows, (4 + len(far) + j) * planes + p] = inverse[a:b, end]
    return SECTION_STEP * own, weights, SECTION_STEP * halo


def azimuth_constants(cells, total):
    root = (np.sqrt(5.0) - 3.0) / 2.0

    def inverse(offset):
        wrapped = sum(np.power(abs(root), np.abs(offset + m * total)) for m in (-1, 0, 1))
        sign = np.where(np.abs(offset) % 2 == 1, -1.0, 1.0)
        return 3.0 / np.sqrt(5.0) * sign * wrapped

    def matrix(offset):
        inner = INNER_A * (inverse(offset + 1) - inverse(offset - 1))
        return inner + INNER_B * (inverse(offset + 2) - inverse(offset - 2))

    ids = np.arange(cells)
    own = matrix(ids[None, :] - ids[:, None])
    weights = np.zeros((16, cells))
    halo = np.zeros((16, cells))
    one = np.ones((), np.int64)
    weights[0] = matrix(1 - (ids - cells)) / inverse(one)
    weights[1, cells - 1] = 1.0
    halo[0] = inverse(ids)
    halo[1, 0] = matrix(one) - inverse(0 * one) * weights[0, cells - 1]
    weights[8] = matrix((cells - 2) - (ids + cells)) / inverse(-one)
    weights[9, 0] = 1.0
    halo[8] = inverse(ids - (cells - 1))
    halo[9, cells - 1] = matrix(-one) - inverse(0 * one) * weights[8, 0]
    return SECTION_STEP * own, weights, SECTION_STEP * halo


def dot(a, b, dims=((1,), (0,))):
    return lax.dot_general(
        a, b, (dims, ((), ())), precision=HIGHEST, preferred_element_type=F32
    )


def kernel(
    n_pln, n_azi, planes, far,
    x_hbm, c_hbm, own_hbm, w_hbm, u_hbm, az_hbm, wa_hbm, ua_hbm, ra_hbm, o_hbm,
    x, c, own, w, u, az, wa, ua, ra,
    h, ha, sb, sa, acc, rad, azd, am, acum, wt, s, g, inc, out,
    load_sem, out_sem, send_sem, recv_sem, asend_sem, arecv_sem, gsend_sem, grecv_sem,
):
    pln = lax.axis_index("pln")
    azi = lax.axis_index("azi")
    rows = x.shape[1]
    cells = x.shape[2]
    pair = 2 * planes
    steps = rows // CHUNK

    loads = []

    def load(src, dst):
        copy = pltpu.make_async_copy(src, dst, load_sem.at[len(loads)])
        copy.start()
        loads.append(copy)
        return copy

    get_w = load(w_hbm.at[pln], w)
    get_x = [load(x_hbm.at[f], x.at[f]) for f in range(5)]
    get_wa = load(wa_hbm, wa)
    get_c = load(c_hbm, c)
    get_own = load(own_hbm.at[pln], own)
    get_az = load(az_hbm, az)
    get_ra = load(ra_hbm, ra)
    get_u = load(u_hbm.at[pln], u)
    get_ua = load(ua_hbm, ua)

    h[...] = jnp.zeros_like(h)

    barrier = pltpu.get_barrier_semaphore()
    distances = (1,) + tuple(far)
    expected = jnp.int32(n_azi - 1)
    for d in distances:
        for sign in (1, -1):
            target = pln + sign * d
            valid = (target >= 0) & (target < n_pln)
            expected = expected + valid.astype(jnp.int32)

            @pl.when(valid)
            def _(target=target):
                pl.semaphore_signal(barrier, 1, device_id={"pln": target}, device_id_type=MESH)

    for d in range(1, n_azi):
        peer = lax.rem(azi + d, n_azi)
        pl.semaphore_signal(barrier, 1, device_id={"azi": peer}, device_id_type=MESH)

    get_w.wait()
    for f in range(5):
        get_x[f].wait()
        sb[f] = dot(w[...], x[f])
    pl.semaphore_wait(barrier, expected)

    transfers = []
    for sign in (1, -1):
        base = 0 if sign == 1 else pair
        for j, d in enumerate(distances):
            if d == 1:
                src = sb.at[:, pl.ds(base, pair)]
                dst = h.at[:, pl.ds(base, pair)]
            else:
                slot = 2 * pair + ((j - 1) + (0 if sign == 1 else len(far))) * planes
                src = sb.at[:, pl.ds(base, planes)]
                dst = h.at[:, pl.ds(slot, planes)]
            target = pln + sign * d
            source = pln - sign * d
            index = len(transfers)
            copy = pltpu.make_async_remote_copy(
                src_ref=src, dst_ref=dst, send_sem=send_sem.at[index],
                recv_sem=recv_sem.at[index], device_id={"pln": target}, device_id_type=MESH,
            )
            sends = (target >= 0) & (target < n_pln)
            receives = (source >= 0) & (source < n_pln)
            transfers.append((d, copy, sends, receives))
    for d, copy, sends, receives in sorted(transfers, key=lambda t: t[0]):

        @pl.when(sends)
        def _(copy=copy):
            copy.start()

    get_wa.wait()
    for f in range(2):
        sa[:, pl.ds(f * rows, rows)] = dot(wa[...], x[3 + f], ((1,), (1,)))
    around = []
    for j, step in enumerate((1, n_azi - 1)):
        copy = pltpu.make_async_remote_copy(
            src_ref=sa.at[pl.ds(8 * j, 8)], dst_ref=ha.at[pl.ds(8 * j, 8)],
            send_sem=asend_sem.at[j], recv_sem=arecv_sem.at[j],
            device_id={"azi": lax.rem(azi + step, n_azi)}, device_id_type=MESH,
        )
        copy.start()
        around.append(copy)

    get_own.wait()
    for f in range(5):
        acc[f] = dot(own[...], x[f])
    get_az.wait()
    for f in range(2):
        azd[f] = dot(x[3 + f], az[...])
    get_ra.wait()
    rad[0] = dot(ra[...], x[2])
    rad[1] = dot(ra[...], x[4])

    lane = lax.broadcasted_iota(jnp.int32, (CHUNK, LANES), 1)
    get_c.wait()

    def rate_step(it, carry):
        at = pl.ds(pl.multiple_of(it * CHUNK, CHUNK), CHUNK)
        halves = []
        for half in range(2):
            cols = pl.ds(half * LANES, LANES)
            e = 1.0 / (1.0 + c[at, cols])
            wt[at, cols] = e
            for k, shift in enumerate(SHIFTS):
                keep = jnp.where(lane >= shift, 1.0 - e, 0.0)
                am[k, at, cols] = keep
                e = e + keep * pltpu.roll(e, shift, 1)
            halves.append(e)
        first, second = halves
        acum[at, pl.ds(0, LANES)] = 1.0 - first
        am[len(SHIFTS), at, pl.ds(0, LANES)] = 1.0 - second
        second = second + (1.0 - second) * first[:, LANES - 1 :]
        acum[at, pl.ds(LANES, LANES)] = 1.0 - second
        s[5, at, pl.ds(LANES, LANES)] = second
        return carry

    lax.fori_loop(0, steps, rate_step, 0)

    get_u.wait()
    get_ua.wait()
    for copy in around:
        copy.wait_recv()
    for f in range(2):
        azd[f] += dot(ha[:, pl.ds(f * rows, rows)], ua[...], ((0,), (0,)))
    for d, copy, sends, receives in transfers:

        @pl.when(receives)
        def _(copy=copy):
            copy.wait_recv()

    for f in range(5):
        acc[f] += dot(u[...], h[f])

    def section_step(it, carry):
        at = pl.ds(pl.multiple_of(it * CHUNK, CHUNK), CHUNK)
        firsts = None
        for half in range(2):
            cols = pl.ds(half * LANES, LANES)
            ax = [acc[f, at, cols] for f in range(5)]
            div = ax[1] + rad[0, at, cols] + azd[0, at, cols]
            other = (div, ax[4], rad[1, at, cols], azd[1, at, cols], div)
            weight = wt[at, cols]
            values = [
                (x[f, at, cols] - MEAN_MACH * ax[f] - other[f]) * weight for f in range(5)
            ]
            for k, shift in enumerate(SHIFTS):
                keep = am[k, at, cols]
                values = [v + keep * pltpu.roll(v, shift, 1) for v in values]
            if half == 1:
                keep = am[len(SHIFTS), at, pl.ds(0, LANES)]
                values = [v + keep * p[:, LANES - 1 :] for v, p in zip(values, firsts)]
            for f in range(5):
                s[f, at, cols] = values[f]
            firsts = values
        return carry

    lax.fori_loop(0, steps, section_step, 0)

    sub = lax.broadcasted_iota(jnp.int32, (8, LANES), 0)
    col = lax.broadcasted_iota(jnp.int32, (8, LANES), 1)
    maps = jnp.zeros((8, rows), F32)
    for q in range(6):
        pick = jnp.where((sub == q) & (col == LANES - 1), 1.0, 0.0)
        maps = maps + dot(pick, s[q, :, pl.ds(LANES, LANES)], ((1,), (1,)))
    g[0] = maps
    gathers = []
    for d in range(1, n_azi):
        copy = pltpu.make_async_remote_copy(
            src_ref=g.at[0], dst_ref=g.at[d], send_sem=gsend_sem.at[d - 1],
            recv_sem=grecv_sem.at[d - 1],
            device_id={"azi": lax.rem(azi + d, n_azi)}, device_id_type=MESH,
        )
        copy.start()
        gathers.append(copy)
    for copy in gathers:
        copy.wait_recv()
    total = g[0]
    for d in range(n_azi - 1, 0, -1):
        block = g[d]
        total = block + (1.0 - block[5:6]) * total
    used = lax.broadcasted_iota(jnp.int32, (8, rows), 0) < 5
    incoming = jnp.where(used, total / total[5:6], 0.0)

    stores = []
    for q in range(5):
        spread = jnp.where(sub == q, 1.0, 0.0)
        inc[...] = dot(incoming, spread, ((0,), (0,)))

        def final_step(it, carry, q=q):
            at = pl.ds(pl.multiple_of(it * CHUNK, CHUNK), CHUNK)
            for half in range(2):
                cols = pl.ds(half * LANES, LANES)
                out[q, at, cols] = s[q, at, cols] + acum[at, cols] * inc[at]
            return carry

        lax.fori_loop(0, steps, final_step, 0, unroll=4)
        copy = pltpu.make_async_copy(out.at[q], o_hbm.at[q], out_sem.at[q])
        copy.start()
        stores.append(copy)

    for d, copy, sends, receives in transfers:

        @pl.when(sends)
        def _(copy=copy):
            copy.wait_send()

    for copy in around + gathers:
        copy.wait_send()
    for copy in stores:
        copy.wait()


def local(fields, swirl_cfl):
    count, planes, axial, cells = fields.shape
    n_pln = lax.axis_size("pln")
    n_azi = lax.axis_size("azi")
    rows = planes * axial
    root = (3.0 - np.sqrt(5.0)) / 2.0
    tiny = float(np.finfo(np.float32).tiny)
    far = [d for d in range(2, n_pln) if 2.0 * root ** (axial * (d - 1)) >= tiny]
    own, weights, halo = axial_constants(planes, axial, n_pln, far)
    azim, azim_weights, azim_halo = azimuth_constants(cells, cells * n_azi)
    radial = SECTION_STEP * np.kron(line_matrices(planes)[1], np.eye(axial))
    constants = [
        jnp.asarray(a, F32) for a in (own, weights, halo, azim, azim_weights, azim_halo, radial)
    ]
    halo_rows = (4 + 2 * len(far)) * planes
    ways = 2 * (1 + len(far))
    vmem = lambda *shape: pltpu.VMEM(shape, F32)
    dma = lambda size: pltpu.SemaphoreType.DMA((size,))
    out = pl.pallas_call(
        functools.partial(kernel, n_pln, n_azi, planes, far),
        out_shape=jax.ShapeDtypeStruct((5, rows, cells), F32),
        in_specs=[pl.BlockSpec(memory_space=pl.ANY)] * 9,
        out_specs=pl.BlockSpec(memory_space=pl.ANY),
        scratch_shapes=[
            vmem(5, rows, cells),
            vmem(rows, cells),
            vmem(rows, rows),
            vmem(4 * planes, rows),
            vmem(rows, halo_rows),
            vmem(cells, cells),
            vmem(16, cells),
            vmem(16, cells),
            vmem(rows, rows),
            vmem(5, halo_rows, cells),
            vmem(16, 2 * rows),
            vmem(5, 4 * planes, cells),
            vmem(16, 2 * rows),
            vmem(5, rows, cells),
            vmem(2, rows, cells),
            vmem(2, rows, cells),
            vmem(len(SHIFTS) + 1, rows, cells),
            vmem(rows, cells),
            vmem(rows, cells),
            vmem(6, rows, cells),
            vmem(n_azi, 8, rows),
            vmem(rows, LANES),
            vmem(5, rows, cells),
            dma(13),
            dma(5),
            dma(ways),
            dma(ways),
            dma(2),
            dma(2),
            dma(n_azi - 1),
            dma(n_azi - 1),
        ],
        compiler_params=pltpu.CompilerParams(
            collective_id=0, has_side_effects=True, vmem_limit_bytes=40 * 1024 * 1024
        ),
    )(fields.reshape(count, rows, cells), swirl_cfl.reshape(rows, cells), *constants)
    return out.reshape(fields.shape)


def solution(mesh):
    placed = (P(None, "grp", "pln", "azi"), P("grp", "pln", "azi"))
    return jax.shard_map(
        local, mesh=mesh, in_specs=placed, out_specs=P(None, "grp", "pln", "azi"), check_vma=False
    )
```

time: 743 us -> 46.1 us (0.06); the launches traced: 730 us -> 45.6 us
  other arithmetic: 380 us -> 0 us
  loops' own time: 143 us -> 0 us
  local copies, waits for them, and re-layouts: 110 us -> 9.83 us
  between operations: 48.2 us -> 0.02 us
  Pallas kernels: 0 us -> 35.8 us
  waiting for transfers between devices: 25.8 us -> 0 us
  starting transfers between devices: 15.8 us -> 0 us
  matrix products: 7.5 us -> 0 us
    sub x13 -> x0, other arithmetic: 244 us -> none  [compact_matrix(): lax.linalg.tridiagonal_solve(lower_diag, diagonal, upper_diag, explicit)]
    another operation x5 -> x0, loops' own time: 143 us -> none  [the longest x4 143 us: compact_matrix(): lax.linalg.tridiagonal_solve(lower_diag, diagonal, upper_diag, explicit)]
    div x17 -> x0, other arithmetic: 86.8 us -> none  [the longest x15 86.8 us: compact_matrix(): lax.linalg.tridiagonal_solve(lower_diag, diagonal, upper_diag, explicit)]
    slice x97 -> x0, local copies, waits for them, and re-layouts: 80 us -> none  [the longest x89 77.1 us: compact_matrix(): lax.linalg.tridiagonal_solve(lower_diag, diagonal, upper_diag, explicit)]
    broadcast_in_dim x18 -> x0, other arithmetic: 40.9 us -> none  [compact_matrix(): lax.linalg.tridiagonal_solve(lower_diag, diagonal, upper_diag, explicit)]
    pallas_call x0 -> x1, Pallas kernels: none -> 35.8 us  [local(): pl.pallas_call(functools.partial(kernel, n_pln, n_azi, planes, far), out_...]
    all_to_all x2 -> x0, waiting for transfers between devices: 21.3 us -> none  [the longest x1 21.3 us: local(): lax.all_to_all(pencils_dx, 'pln', split_axis=2, concat_axis=1, tiled=True)]
    all_to_all x2 -> x0, starting transfers between devices: 11.5 us -> none  [the longest x1 6.45 us: local(): lax.all_to_all(fields, 'pln', split_axis=1, concat_axis=2, tiled=True)]
  transfers between devices with their start and end apart: 7 -> 0, of which waited for: 4 -> 0; matrix products, arithmetic and copies ran while one was open for 65% -> 0% of each run, Pallas kernels for 0% -> 0%
where the time goes in v1:
time: 46.1 us; the launch traced here: 45.6 us
  Pallas kernels  35.8 us (78%)
  local copies, waits for them, and re-layouts  9.83 us (21%)
    pallas_call x1, Pallas kernels, local(): pl.pallas_call(functools.partial(kernel, n_pln, n_azi, planes, far), out_...  35.8 us
    unnamed x19, local copies, waits for them, and re-layouts  9.83 us

profile of v1, /device:TPU:0, one launch (start us, length us, event | category | flops | bytes accessed | tf_op | source)
XLA Modules:
  0.0 45.6 jit_solution(465410099604823258)
XLA Ops:
  0.0 0.0 copy-start
  0.0 1.3 %copy-done = f32[5,8,32,256]{3,2,1,0:T(8,128)S(1)} copy-done((f32[5,8,32,256]{3,2,1,0:T(8,128)S(1)}, f32[5,8,32,256]{3,2,1,0:T(8,128)}, u32[]{:S(2)}) %copy-start) | copy-done | bytes 1310744
  1.3 0.0 copy-start.1
  1.3 1.2 %copy-done.1 = f32[4,256,256]{2,1,0:T(8,128)S(1)} copy-done((f32[4,256,256]{2,1,0:T(8,128)S(1)}, f32[4,256,256]{2,1,0:T(8,128)}, u32[]{:S(2)}) %copy-start.1) | copy-done | bytes 1048600
  2.5 0.0 copy-start.2
  2.5 1.0 %copy-done.2 = f32[4,256,64]{2,1,0:T(8,128)S(1)} copy-done((f32[4,256,64]{2,1,0:T(8,128)S(1)}, f32[4,256,64]{2,1,0:T(8,128)}, u32[]{:S(2)}) %copy-start.2) | copy-done | bytes 262168
  3.6 0.0 copy-start.3
  3.6 0.9 %copy-done.3 = f32[8,32,256]{2,1,0:T(8,128)S(1)} copy-done((f32[8,32,256]{2,1,0:T(8,128)S(1)}, f32[8,32,256]{2,1,0:T(8,128)}, u32[]{:S(2)}) %copy-start.3) | copy-done | bytes 262168
  4.5 0.0 copy-start.4
  4.5 0.9 %copy-done.4 = f32[256,256]{1,0:T(8,128)S(1)} copy-done((f32[256,256]{1,0:T(8,128)S(1)}, f32[256,256]{1,0:T(8,128)}, u32[]{:S(2)}) %copy-start.4) | copy-done | bytes 262168
  5.5 0.0 copy-start.5
  5.5 0.9 %copy-done.5 = f32[256,256]{1,0:T(8,128)S(1)} copy-done((f32[256,256]{1,0:T(8,128)S(1)}, f32[256,256]{1,0:T(8,128)}, u32[]{:S(2)}) %copy-start.5) | copy-done | bytes 262168
  6.4 0.0 copy-start.6
  6.4 0.9 %copy-done.6 = f32[4,32,256]{2,1,0:T(8,128)S(1)} copy-done((f32[4,32,256]{2,1,0:T(8,128)S(1)}, f32[4,32,256]{2,1,0:T(8,128)}, u32[]{:S(2)}) %copy-start.6) | copy-done | bytes 131096
  7.3 0.0 copy-start.7
  7.3 0.7 %copy-done.7 = f32[16,256]{1,0:T(8,128)S(1)} copy-done((f32[16,256]{1,0:T(8,128)S(1)}, f32[16,256]{1,0:T(8,128)}, u32[]{:S(2)}) %copy-start.7) | copy-done | bytes 16408
  8.1 0.0 copy-start.8
  8.1 0.7 %copy-done.8 = f32[16,256]{1,0:T(8,128)S(1)} copy-done((f32[16,256]{1,0:T(8,128)S(1)}, f32[16,256]{1,0:T(8,128)}, u32[]{:S(2)}) %copy-start.8) | copy-done | bytes 16408
  8.8 35.8 %shard_map.91 = f32[5,256,256]{2,1,0:T(8,128)S(1)} custom-call(f32[5,256,256]{2,1,0:T(8,128)S(1)} %bitcast.4, f32[256,256]{1,0:T(8,128)S(1)} %bitcast.5, f32[4,256,256]{2,1,0:T(8,128)S(1)} %copy-done.1, f32[4,32,256]{2,1,0:T(8,128)S(1)} %copy-done.6, f32[4,256,64]{2,1,0:T(8,128)S(1)} %copy-done.2, f32[256,256]{1,0:T(8,128)S(1)} %copy-done.5, ...), custom_call_target="tpu_custom_call" | custom-call | tf_op jit(solution)/shard_map/pallas_call | solution.py:369
  44.6 1.1 %copy.11 = f32[5,8,32,256]{3,2,1,0:T(8,128)} copy(f32[5,8,32,256]{3,2,1,0:T(8,128)S(1)} %bitcast.3) | data formatting | bytes 2621440
Async XLA Ops:
  0.0 1.3 %copy-start = (f32[5,8,32,256]{3,2,1,0:T(8,128)S(1)}, f32[5,8,32,256]{3,2,1,0:T(8,128)}, u32[]{:S(2)}) copy-start(f32[5,8,32,256]{3,2,1,0:T(8,128)} %param.9) | copy-start | bytes 3932164
  1.3 1.2 %copy-start.1 = (f32[4,256,256]{2,1,0:T(8,128)S(1)}, f32[4,256,256]{2,1,0:T(8,128)}, u32[]{:S(2)}) copy-start(f32[4,256,256]{2,1,0:T(8,128)} %constant.14.clone.own_hbm) | copy-start | bytes 3145732
  2.5 1.0 %copy-start.2 = (f32[4,256,64]{2,1,0:T(8,128)S(1)}, f32[4,256,64]{2,1,0:T(8,128)}, u32[]{:S(2)}) copy-start(f32[4,256,64]{2,1,0:T(8,128)} %constant.16.clone.u_hbm) | copy-start | bytes 786436
  3.6 0.9 %copy-start.3 = (f32[8,32,256]{2,1,0:T(8,128)S(1)}, f32[8,32,256]{2,1,0:T(8,128)}, u32[]{:S(2)}) copy-start(f32[8,32,256]{2,1,0:T(8,128)} %param.10) | copy-start | bytes 786436
  4.5 0.9 %copy-start.4 = (f32[256,256]{1,0:T(8,128)S(1)}, f32[256,256]{1,0:T(8,128)}, u32[]{:S(2)}) copy-start(f32[256,256]{1,0:T(8,128)} %constant.20.clone.ra_hbm) | copy-start | bytes 786436
  5.5 0.9 %copy-start.5 = (f32[256,256]{1,0:T(8,128)S(1)}, f32[256,256]{1,0:T(8,128)}, u32[]{:S(2)}) copy-start(f32[256,256]{1,0:T(8,128)} %constant.17.clone.az_hbm) | copy-start | bytes 786436
  6.4 0.9 %copy-start.6 = (f32[4,32,256]{2,1,0:T(8,128)S(1)}, f32[4,32,256]{2,1,0:T(8,128)}, u32[]{:S(2)}) copy-start(f32[4,32,256]{2,1,0:T(8,128)} %constant.15.clone.w_hbm) | copy-start | bytes 393220
  7.3 0.7 %copy-start.7 = (f32[16,256]{1,0:T(8,128)S(1)}, f32[16,256]{1,0:T(8,128)}, u32[]{:S(2)}) copy-start(f32[16,256]{1,0:T(8,128)} %constant.19.clone.ua_hbm) | copy-start | bytes 49156
  8.1 0.7 %copy-start.8 = (f32[16,256]{1,0:T(8,128)S(1)}, f32[16,256]{1,0:T(8,128)}, u32[]{:S(2)}) copy-start(f32[16,256]{1,0:T(8,128)} %constant.18.clone.wa_hbm) | copy-start | bytes 49156

commit v2 on v1

--- a/solution.py
+++ b/solution.py
@@ -12,11 +12,12 @@
 INNER_B = 1.0 / 36.0
 MEAN_MACH = 0.4
 SECTION_STEP = 0.25
-HIGHEST = lax.Precision.HIGHEST
+THREE_PASS = lax.Precision.HIGH
 MESH = pl.DeviceIdType.MESH
 F32 = jnp.float32
 LANES = 128
-CHUNK = 16
+CHUNK = 64
+RATE_CHUNK = 64
 SHIFTS = (1, 2, 4, 8, 16, 32, 64)
 
 
@@ -118,7 +119,7 @@
 
 def dot(a, b, dims=((1,), (0,))):
     return lax.dot_general(
-        a, b, (dims, ((), ())), precision=HIGHEST, preferred_element_type=F32
+        a, b, (dims, ((), ())), precision=THREE_PASS, preferred_element_type=F32
     )
 
 
@@ -229,30 +230,29 @@
     rad[0] = dot(ra[...], x[2])
     rad[1] = dot(ra[...], x[4])
 
-    lane = lax.broadcasted_iota(jnp.int32, (CHUNK, LANES), 1)
+    lane = lax.broadcasted_iota(jnp.int32, (RATE_CHUNK, LANES), 1)
+    halves = [pl.ds(half * LANES, LANES) for half in range(2)]
     get_c.wait()
 
     def rate_step(it, carry):
-        at = pl.ds(pl.multiple_of(it * CHUNK, CHUNK), CHUNK)
-        halves = []
-        for half in range(2):
-            cols = pl.ds(half * LANES, LANES)
-            e = 1.0 / (1.0 + c[at, cols])
+        at = pl.ds(pl.multiple_of(it * RATE_CHUNK, RATE_CHUNK), RATE_CHUNK)
+        parts = [1.0 / (1.0 + c[at, cols]) for cols in halves]
+        for cols, e in zip(halves, parts):
             wt[at, cols] = e
-            for k, shift in enumerate(SHIFTS):
-                keep = jnp.where(lane >= shift, 1.0 - e, 0.0)
+        for k, shift in enumerate(SHIFTS):
+            keeps = [jnp.where(lane >= shift, 1.0 - e, 0.0) for e in parts]
+            for cols, keep in zip(halves, keeps):
                 am[k, at, cols] = keep
-                e = e + keep * pltpu.roll(e, shift, 1)
-            halves.append(e)
-        first, second = halves
-        acum[at, pl.ds(0, LANES)] = 1.0 - first
-        am[len(SHIFTS), at, pl.ds(0, LANES)] = 1.0 - second
+            parts = [e + keep * pltpu.roll(e, shift, 1) for e, keep in zip(parts, keeps)]
+        first, second = parts
+        acum[at, halves[0]] = 1.0 - first
+        am[len(SHIFTS), at, halves[0]] = 1.0 - second
         second = second + (1.0 - second) * first[:, LANES - 1 :]
-        acum[at, pl.ds(LANES, LANES)] = 1.0 - second
-        s[5, at, pl.ds(LANES, LANES)] = second
+        acum[at, halves[1]] = 1.0 - second
+        s[5, at, halves[1]] = second
         return carry
 
-    lax.fori_loop(0, steps, rate_step, 0)
+    lax.fori_loop(0, rows // RATE_CHUNK, rate_step, 0)
 
     get_u.wait()
     get_ua.wait()
@@ -271,25 +271,24 @@
 
     def section_step(it, carry):
         at = pl.ds(pl.multiple_of(it * CHUNK, CHUNK), CHUNK)
-        firsts = None
-        for half in range(2):
-            cols = pl.ds(half * LANES, LANES)
+        parts = []
+        for cols in halves:
             ax = [acc[f, at, cols] for f in range(5)]
             div = ax[1] + rad[0, at, cols] + azd[0, at, cols]
             other = (div, ax[4], rad[1, at, cols], azd[1, at, cols], div)
             weight = wt[at, cols]
-            values = [
-                (x[f, at, cols] - MEAN_MACH * ax[f] - other[f]) * weight for f in range(5)
+            parts.append(
+                [(x[f, at, cols] - MEAN_MACH * ax[f] - other[f]) * weight for f in range(5)]
+            )
+        for k, shift in enumerate(SHIFTS):
+            parts = [
+                [v + am[k, at, cols] * pltpu.roll(v, shift, 1) for v in values]
+                for cols, values in zip(halves, parts)
             ]
-            for k, shift in enumerate(SHIFTS):
-                keep = am[k, at, cols]
-                values = [v + keep * pltpu.roll(v, shift, 1) for v in values]
-            if half == 1:
-                keep = am[len(SHIFTS), at, pl.ds(0, LANES)]
-                values = [v + keep * p[:, LANES - 1 :] for v, p in zip(values, firsts)]
-            for f in range(5):
-                s[f, at, cols] = values[f]
-            firsts = values
+        keep = am[len(SHIFTS), at, halves[0]]
+        for f in range(5):
+            s[f, at, halves[0]] = parts[0][f]
+            s[f, at, halves[1]] = parts[1][f] + keep * parts[0][f][:, LANES - 1 :]
         return carry
 
     lax.fori_loop(0, steps, section_step, 0)
@@ -326,12 +325,11 @@
 
         def final_step(it, carry, q=q):
             at = pl.ds(pl.multiple_of(it * CHUNK, CHUNK), CHUNK)
-            for half in range(2):
-                cols = pl.ds(half * LANES, LANES)
+            for cols in halves:
                 out[q, at, cols] = s[q, at, cols] + acum[at, cols] * inc[at]
             return carry
 
-        lax.fori_loop(0, steps, final_step, 0, unroll=4)
+        lax.fori_loop(0, steps, final_step, 0, unroll=2)
         copy = pltpu.make_async_copy(out.at[q], o_hbm.at[q], out_sem.at[q])
         copy.start()
         stores.append(copy)
@@ -405,7 +403,7 @@
             dma(n_azi - 1),
         ],
         compiler_params=pltpu.CompilerParams(
-            collective_id=0, has_side_effects=True, vmem_limit_bytes=40 * 1024 * 1024
+            collective_id=0, has_side_effects=True, vmem_limit_bytes=60 * 1024 * 1024
         ),
     )(fields.reshape(count, rows, cells), swirl_cfl.reshape(rows, cells), *constants)
     return out.reshape(fields.shape)

time: 46.1 us -> 24 us (0.52)
  Pallas kernels: 35.8 us -> 21.3 us
  local copies, waits for them, and re-layouts: 9.83 us -> 2.52 us
    pallas_call x1, Pallas kernels: 35.8 us -> 21.3 us  [local(): pl.pallas_call(functools.partial(kernel, n_pln, n_azi, planes, far), out_...]
    unnamed x19 -> x1, local copies, waits for them, and re-layouts: 9.83 us -> 2.52 us
where the time goes in v2:
time: 24 us; the launch traced here: 23.8 us
  Pallas kernels  21.3 us (89%)
  local copies, waits for them, and re-layouts  2.52 us (10%)
    pallas_call x1, Pallas kernels, local(): pl.pallas_call(functools.partial(kernel, n_pln, n_azi, planes, far), out_...  21.3 us
    unnamed x1, local copies, waits for them, and re-layouts  2.52 us

profile of v2, /device:TPU:0, one launch (start us, length us, event | category | flops | bytes accessed | tf_op | source)
XLA Modules:
  0.0 23.8 jit_solution(13520341091609627984)
XLA Ops:
  0.0 21.3 %shard_map.91 = f32[5,256,256]{2,1,0:T(8,128)} custom-call(f32[5,256,256]{2,1,0:T(8,128)} %bitcast.4, f32[256,256]{1,0:T(8,128)} %bitcast.5, f32[4,256,256]{2,1,0:T(8,128)} %constant.14.clone.own_hbm, f32[4,32,256]{2,1,0:T(8,128)} %constant.15.clone.w_hbm, f32[4,256,64]{2,1,0:T(8,128)} %constant.16.clone.u_hbm, f32[256,256]{1,0:T(8,128)} %constant.17.clone.az_hbm, ...), custom_call_target="tpu_custom_call" | custom-call | tf_op jit(solution)/shard_map/pallas_call | solution.py:367
  21.3 2.5 %copy.11 = f32[5,8,32,256]{3,2,1,0:T(8,128)} copy(f32[5,8,32,256]{3,2,1,0:T(8,128)} %bitcast.3) | data formatting | bytes 2621440

commit v3 on v2

--- a/solution.py
+++ b/solution.py
@@ -17,7 +17,6 @@
 F32 = jnp.float32
 LANES = 128
 CHUNK = 64
-RATE_CHUNK = 64
 SHIFTS = (1, 2, 4, 8, 16, 32, 64)
 
 
@@ -125,9 +124,9 @@
 
 def kernel(
     n_pln, n_azi, planes, far,
-    x_hbm, c_hbm, own_hbm, w_hbm, u_hbm, az_hbm, wa_hbm, ua_hbm, ra_hbm, o_hbm,
+    x_hbm, c_hbm, own_hbm, w_hbm, u_hbm, az_hbm, wa_hbm, ua_hbm, ra_hbm, s_hbm, acum_hbm, inc_hbm,
     x, c, own, w, u, az, wa, ua, ra,
-    h, ha, sb, sa, acc, rad, azd, am, acum, wt, s, g, inc, out,
+    h, ha, sb, sa, acc, rad, azd, am, acum, wt, s, g, inc,
     load_sem, out_sem, send_sem, recv_sem, asend_sem, arecv_sem, gsend_sem, grecv_sem,
 ):
     pln = lax.axis_index("pln")
@@ -174,38 +173,51 @@
         peer = lax.rem(azi + d, n_azi)
         pl.semaphore_signal(barrier, 1, device_id={"azi": peer}, device_id_type=MESH)
 
-    get_w.wait()
-    for f in range(5):
-        get_x[f].wait()
-        sb[f] = dot(w[...], x[f])
-    pl.semaphore_wait(barrier, expected)
-
     transfers = []
     for sign in (1, -1):
         base = 0 if sign == 1 else pair
         for j, d in enumerate(distances):
             if d == 1:
-                src = sb.at[:, pl.ds(base, pair)]
-                dst = h.at[:, pl.ds(base, pair)]
+                src_rows, dst_rows = pl.ds(base, pair), pl.ds(base, pair)
             else:
                 slot = 2 * pair + ((j - 1) + (0 if sign == 1 else len(far))) * planes
-                src = sb.at[:, pl.ds(base, planes)]
-                dst = h.at[:, pl.ds(slot, planes)]
+                src_rows, dst_rows = pl.ds(base, planes), pl.ds(slot, planes)
             target = pln + sign * d
             source = pln - sign * d
-            index = len(transfers)
-            copy = pltpu.make_async_remote_copy(
-                src_ref=src, dst_ref=dst, send_sem=send_sem.at[index],
-                recv_sem=recv_sem.at[index], device_id={"pln": target}, device_id_type=MESH,
-            )
             sends = (target >= 0) & (target < n_pln)
             receives = (source >= 0) & (source < n_pln)
-            transfers.append((d, copy, sends, receives))
-    for d, copy, sends, receives in sorted(transfers, key=lambda t: t[0]):
-
-        @pl.when(sends)
-        def _(copy=copy):
-            copy.start()
+            fields = [pl.ds(f, 1) for f in range(5)] if d == 1 else [pl.ds(0, 5)]
+            copies = []
+            for part in fields:
+                index = sum(len(other[1]) for other in transfers) + len(copies)
+                copies.append(
+                    pltpu.make_async_remote_copy(
+                        src_ref=sb.at[part, src_rows], dst_ref=h.at[part, dst_rows],
+                        send_sem=send_sem.at[index], recv_sem=recv_sem.at[index],
+                        device_id={"pln": target}, device_id_type=MESH,
+                    )
+                )
+            transfers.append((d, copies, sends, receives))
+
+    get_w.wait()
+    for f in range(5):
+        get_x[f].wait()
+        sb[f] = dot(w[...], x[f])
+        if f == 0:
+            pl.semaphore_wait(barrier, expected)
+        for d, copies, sends, receives in transfers:
+            if d == 1:
+
+                @pl.when(sends)
+                def _(copies=copies, f=f):
+                    copies[f].start()
+
+    for d, copies, sends, receives in sorted(transfers, key=lambda t: t[0]):
+        if d > 1:
+
+            @pl.when(sends)
+            def _(copies=copies):
+                copies[0].start()
 
     get_wa.wait()
     for f in range(2):
@@ -230,12 +242,22 @@
     rad[0] = dot(ra[...], x[2])
     rad[1] = dot(ra[...], x[4])
 
-    lane = lax.broadcasted_iota(jnp.int32, (RATE_CHUNK, LANES), 1)
+    lane = lax.broadcasted_iota(jnp.int32, (CHUNK, LANES), 1)
+    line = lax.broadcasted_iota(jnp.int32, (CHUNK, LANES), 0)
+    per_tile = LANES // CHUNK
+
+    def note_end(it, q, values):
+        tile = lax.div(it, per_tile)
+        here = lane == line + CHUNK * lax.rem(it, per_tile)
+        ends = jnp.where(here, jnp.broadcast_to(values[:, LANES - 1 :], here.shape), 0.0)
+        g[0, tile, q : q + 1] += jnp.sum(ends, axis=0, keepdims=True)
+
+    g[0] = jnp.zeros(g.shape[1:], F32)
     halves = [pl.ds(half * LANES, LANES) for half in range(2)]
     get_c.wait()
 
     def rate_step(it, carry):
-        at = pl.ds(pl.multiple_of(it * RATE_CHUNK, RATE_CHUNK), RATE_CHUNK)
+        at = pl.ds(pl.multiple_of(it * CHUNK, CHUNK), CHUNK)
         parts = [1.0 / (1.0 + c[at, cols]) for cols in halves]
         for cols, e in zip(halves, parts):
             wt[at, cols] = e
@@ -249,10 +271,13 @@
         am[len(SHIFTS), at, halves[0]] = 1.0 - second
         second = second + (1.0 - second) * first[:, LANES - 1 :]
         acum[at, halves[1]] = 1.0 - second
-        s[5, at, halves[1]] = second
+        note_end(it, 5, second)
         return carry
 
-    lax.fori_loop(0, rows // RATE_CHUNK, rate_step, 0)
+    lax.fori_loop(0, rows // CHUNK, rate_step, 0)
+
+    put_acum = pltpu.make_async_copy(acum, acum_hbm, out_sem.at[5])
+    put_acum.start()
 
     get_u.wait()
     get_ua.wait()
@@ -260,11 +285,12 @@
         copy.wait_recv()
     for f in range(2):
         azd[f] += dot(ha[:, pl.ds(f * rows, rows)], ua[...], ((0,), (0,)))
-    for d, copy, sends, receives in transfers:
+    for d, copies, sends, receives in transfers:
 
         @pl.when(receives)
-        def _(copy=copy):
-            copy.wait_recv()
+        def _(copies=copies):
+            for copy in copies:
+                copy.wait_recv()
 
     for f in range(5):
         acc[f] += dot(u[...], h[f])
@@ -288,18 +314,13 @@
         keep = am[len(SHIFTS), at, halves[0]]
         for f in range(5):
             s[f, at, halves[0]] = parts[0][f]
-            s[f, at, halves[1]] = parts[1][f] + keep * parts[0][f][:, LANES - 1 :]
+            second = parts[1][f] + keep * parts[0][f][:, LANES - 1 :]
+            s[f, at, halves[1]] = second
+            note_end(it, f, second)
         return carry
 
     lax.fori_loop(0, steps, section_step, 0)
 
-    sub = lax.broadcasted_iota(jnp.int32, (8, LANES), 0)
-    col = lax.broadcasted_iota(jnp.int32, (8, LANES), 1)
-    maps = jnp.zeros((8, rows), F32)
-    for q in range(6):
-        pick = jnp.where((sub == q) & (col == LANES - 1), 1.0, 0.0)
-        maps = maps + dot(pick, s[q, :, pl.ds(LANES, LANES)], ((1,), (1,)))
-    g[0] = maps
     gathers = []
     for d in range(1, n_azi):
         copy = pltpu.make_async_remote_copy(
@@ -309,39 +330,62 @@
         )
         copy.start()
         gathers.append(copy)
+    stores = [put_acum]
+    for f in range(5):
+        copy = pltpu.make_async_copy(s.at[f], s_hbm.at[f], out_sem.at[f])
+        copy.start()
+        stores.append(copy)
     for copy in gathers:
         copy.wait_recv()
     total = g[0]
     for d in range(n_azi - 1, 0, -1):
         block = g[d]
-        total = block + (1.0 - block[5:6]) * total
-    used = lax.broadcasted_iota(jnp.int32, (8, rows), 0) < 5
-    incoming = jnp.where(used, total / total[5:6], 0.0)
-
-    stores = []
-    for q in range(5):
-        spread = jnp.where(sub == q, 1.0, 0.0)
-        inc[...] = dot(incoming, spread, ((0,), (0,)))
-
-        def final_step(it, carry, q=q):
-            at = pl.ds(pl.multiple_of(it * CHUNK, CHUNK), CHUNK)
-            for cols in halves:
-                out[q, at, cols] = s[q, at, cols] + acum[at, cols] * inc[at]
-            return carry
-
-        lax.fori_loop(0, steps, final_step, 0, unroll=2)
-        copy = pltpu.make_async_copy(out.at[q], o_hbm.at[q], out_sem.at[q])
-        copy.start()
-        stores.append(copy)
-
-    for d, copy, sends, receives in transfers:
+        total = block + (1.0 - block[:, 5:6]) * total
+    used = lax.broadcasted_iota(jnp.int32, total.shape, 1) < 5
+    inc[...] = jnp.where(used, total / total[:, 5:6], 0.0)
+    put_inc = pltpu.make_async_copy(inc, inc_hbm, out_sem.at[6])
+    put_inc.start()
+
+    for d, copies, sends, receives in transfers:
 
         @pl.when(sends)
-        def _(copy=copy):
-            copy.wait_send()
+        def _(copies=copies):
+            for copy in copies:
+                copy.wait_send()
 
     for copy in around + gathers:
         copy.wait_send()
+    for copy in stores + [put_inc]:
+        copy.wait()
+
+
+def advance(
+    s_hbm, acum_hbm, inc_hbm, o_hbm, s, acum, inc, wide, out, load_sem, out_sem
+):
+    loads = [
+        pltpu.make_async_copy(inc_hbm, inc, load_sem.at[5]),
+        pltpu.make_async_copy(acum_hbm, acum, load_sem.at[6]),
+    ]
+    loads += [pltpu.make_async_copy(s_hbm.at[f], s.at[f], load_sem.at[f]) for f in range(5)]
+    for copy in loads:
+        copy.start()
+    rows = s.shape[1]
+    loads[0].wait()
+    sub = lax.broadcasted_iota(jnp.int32, (8, 5 * LANES), 0)
+    col = lax.broadcasted_iota(jnp.int32, (8, 5 * LANES), 1)
+    spread = jnp.where((col >= sub * LANES) & (col < (sub + 1) * LANES), 1.0, 0.0)
+    for tile in range(rows // LANES):
+        wide[pl.ds(tile * LANES, LANES)] = dot(inc[tile], spread, ((0,), (0,)))
+    loads[1].wait()
+    stores = []
+    for f in range(5):
+        loads[2 + f].wait()
+        for half in range(2):
+            cols = pl.ds(half * LANES, LANES)
+            out[f, :, cols] = s[f, :, cols] + acum[:, cols] * wide[:, pl.ds(f * LANES, LANES)]
+        copy = pltpu.make_async_copy(out.at[f], o_hbm.at[f], out_sem.at[f])
+        copy.start()
+        stores.append(copy)
     for copy in stores:
         copy.wait()
 
@@ -361,14 +405,17 @@
         jnp.asarray(a, F32) for a in (own, weights, halo, azim, azim_weights, azim_halo, radial)
     ]
     halo_rows = (4 + 2 * len(far)) * planes
-    ways = 2 * (1 + len(far))
+    ways = 2 * (5 + len(far))
     vmem = lambda *shape: pltpu.VMEM(shape, F32)
     dma = lambda size: pltpu.SemaphoreType.DMA((size,))
-    out = pl.pallas_call(
+    shape = lambda *sizes: jax.ShapeDtypeStruct(sizes, F32)
+    tiles = rows // LANES
+    anywhere = pl.BlockSpec(memory_space=pl.ANY)
+    partial, rates, incoming = pl.pallas_call(
         functools.partial(kernel, n_pln, n_azi, planes, far),
-        out_shape=jax.ShapeDtypeStruct((5, rows, cells), F32),
-        in_specs=[pl.BlockSpec(memory_space=pl.ANY)] * 9,
-        out_specs=pl.BlockSpec(memory_space=pl.ANY),
+        out_shape=(shape(5, rows, cells), shape(rows, cells), shape(tiles, 8, LANES)),
+        in_specs=[anywhere] * 9,
+        out_specs=[anywhere] * 3,
         scratch_shapes=[
             vmem(5, rows, cells),
             vmem(rows, cells),
@@ -389,12 +436,11 @@
             vmem(len(SHIFTS) + 1, rows, cells),
             vmem(rows, cells),
             vmem(rows, cells),
-            vmem(6, rows, cells),
-            vmem(n_azi, 8, rows),
-            vmem(rows, LANES),
             vmem(5, rows, cells),
+            vmem(n_azi, tiles, 8, LANES),
+            vmem(tiles, 8, LANES),
             dma(13),
-            dma(5),
+            dma(7),
             dma(ways),
             dma(ways),
             dma(2),
@@ -406,6 +452,22 @@
             collective_id=0, has_side_effects=True, vmem_limit_bytes=60 * 1024 * 1024
         ),
     )(fields.reshape(count, rows, cells), swirl_cfl.reshape(rows, cells), *constants)
+    out = pl.pallas_call(
+        advance,
+        out_shape=shape(5, rows, cells),
+        in_specs=[anywhere] * 3,
+        out_specs=anywhere,
+        scratch_shapes=[
+            vmem(5, rows, cells),
+            vmem(rows, cells),
+            vmem(tiles, 8, LANES),
+            vmem(rows, 5 * LANES),
+            vmem(5, rows, cells),
+            dma(7),
+            dma(5),
+        ],
+        compiler_params=pltpu.CompilerParams(vmem_limit_bytes=60 * 1024 * 1024),
+    )(partial, rates, incoming)
     return out.reshape(fields.shape)
 
 

time: 24 us -> 22.3 us (0.929)
  local copies, waits for them, and re-layouts: 2.52 us -> 0 us
  Pallas kernels: 21.3 us -> 22.1 us
    unnamed x1 -> x0, local copies, waits for them, and re-layouts: 2.52 us -> none
    pallas_call x0 -> x1, Pallas kernels: none -> 2.35 us  [local(): pl.pallas_call(advance, out_shape=shape(5, rows, cells), in_specs=[anywhe...]
    pallas_call x1, Pallas kernels: 21.3 us -> 19.8 us  [local(): pl.pallas_call(functools.partial(kernel, n_pln, n_azi, planes, far), out_...]
where the time goes in v3:
time: 22.3 us; the launch traced here: 22.1 us
  Pallas kernels  22.1 us (99%)
    pallas_call x1, Pallas kernels, local(): pl.pallas_call(functools.partial(kernel, n_pln, n_azi, planes, far), out_...  19.8 us
    pallas_call x1, Pallas kernels, local(): pl.pallas_call(advance, out_shape=shape(5, rows, cells), in_specs=[anywhe...  2.35 us

profile of v3, /device:TPU:0, one launch (start us, length us, event | category | flops | bytes accessed | tf_op | source)
XLA Modules:
  0.0 22.1 jit_solution(7924540294166000315)
XLA Ops:
  0.0 19.8 %shard_map.91 = (f32[5,256,256]{2,1,0:T(8,128)}, f32[256,256]{1,0:T(8,128)}, f32[2,8,128]{2,1,0:T(8,128)}) custom-call(f32[5,256,256]{2,1,0:T(8,128)} %bitcast.3, f32[256,256]{1,0:T(8,128)} %bitcast.4, f32[4,256,256]{2,1,0:T(8,128)} %constant.14.clone.own_hbm, f32[4,32,256]{2,1,0:T(8,128)} %constant.15.clone.w_hbm, f32[4,256,64]{2,1,0:T(8,128)} %constant.16.clone.u_hbm, ...), custom_call_target="tpu_custom_call" | custom-call | tf_op jit(solution)/shard_map/pallas_call | solution.py:414
  19.8 2.3 %shard_map.92 = f32[5,256,256]{2,1,0:T(8,128)} custom-call(f32[5,256,256]{2,1,0:T(8,128)} %get-tuple-element.8.s_hbm, f32[256,256]{1,0:T(8,128)} %get-tuple-element.9.acum_hbm, f32[2,8,128]{2,1,0:T(8,128)} %get-tuple-element.10.inc_hbm), custom_call_target="tpu_custom_call" | custom-call | tf_op jit(solution)/shard_map/pallas_call | solution.py:455

commit v4 on v3

--- a/solution.py
+++ b/solution.py
@@ -16,7 +16,7 @@
 MESH = pl.DeviceIdType.MESH
 F32 = jnp.float32
 LANES = 128
-CHUNK = 64
+CHUNK = 128
 SHIFTS = (1, 2, 4, 8, 16, 32, 64)
 
 
@@ -319,7 +319,7 @@
             note_end(it, f, second)
         return carry
 
-    lax.fori_loop(0, steps, section_step, 0)
+    lax.fori_loop(0, steps, section_step, 0, unroll=2)
 
     gathers = []
     for d in range(1, n_azi):

time: 22.3 us -> 21.1 us (0.946)
  Pallas kernels: 22.1 us -> 20.9 us
    pallas_call x1, Pallas kernels: 19.8 us -> 18.6 us  [local(): pl.pallas_call(functools.partial(kernel, n_pln, n_azi, planes, far), out_...]
where the time goes in v4:
time: 21.1 us; the launch traced here: 20.9 us
  Pallas kernels  20.9 us (99%)
    pallas_call x1, Pallas kernels, local(): pl.pallas_call(functools.partial(kernel, n_pln, n_azi, planes, far), out_...  18.6 us
    pallas_call x1, Pallas kernels, local(): pl.pallas_call(advance, out_shape=shape(5, rows, cells), in_specs=[anywhe...  2.35 us

profile of v4, /device:TPU:0, one launch (start us, length us, event | category | flops | bytes accessed | tf_op | source)
XLA Modules:
  0.0 20.9 jit_solution(3892659209707613323)
XLA Ops:
  0.0 18.6 %shard_map.91 = (f32[5,256,256]{2,1,0:T(8,128)}, f32[256,256]{1,0:T(8,128)}, f32[2,8,128]{2,1,0:T(8,128)}) custom-call(f32[5,256,256]{2,1,0:T(8,128)} %bitcast.3, f32[256,256]{1,0:T(8,128)} %bitcast.4, f32[4,256,256]{2,1,0:T(8,128)} %constant.14.clone.own_hbm, f32[4,32,256]{2,1,0:T(8,128)} %constant.15.clone.w_hbm, f32[4,256,64]{2,1,0:T(8,128)} %constant.16.clone.u_hbm, ...), custom_call_target="tpu_custom_call" | custom-call | tf_op jit(solution)/shard_map/pallas_call | solution.py:414
  18.6 2.4 %shard_map.92 = f32[5,256,256]{2,1,0:T(8,128)} custom-call(f32[5,256,256]{2,1,0:T(8,128)} %get-tuple-element.8.s_hbm, f32[256,256]{1,0:T(8,128)} %get-tuple-element.9.acum_hbm, f32[2,8,128]{2,1,0:T(8,128)} %get-tuple-element.10.inc_hbm), custom_call_target="tpu_custom_call" | custom-call | tf_op jit(solution)/shard_map/pallas_call | solution.py:455
